TPU v7x, 32 devices: a whole 2x2x4 slice. The times are simulated.
32 devices in a mesh: rows: 8 (over y, x, core), section: 4 (over z).
Axes of the slice: x: 2, y: 2, z: 4, core: 2. Of those that a mesh axis runs over, the one named last changes fastest.
Arguments:
- start_vec: float32 [16384, 2, 256], P('rows'), may hold values from -6 to 6
- left_vec: float32 [16384, 2, 256], P('rows'), may hold values from -6 to 6
- hamil: bfloat16 [128, 16, 2, 128, 128], P('rows', 'section'), may hold values from -0.109375 to 0.109375
- cols: int32 [128, 16], P('rows', 'section'), may hold values from 0 to 127, as said below
- live: int32 [128, 4], P('rows', 'section'), may hold values from 1 to 4, as said below
Outputs:
- moments: float32 [5, 256], replicated
- last_vec: float32 [16384, 2, 256], P('rows')
- before_vec: float32 [16384, 2, 256], P('rows')
Inputs may be any that keep to these rules, and one draw needn't show every extreme that they name: `cols`: each block column lies within 16 of its block row; slot 0 of every block row is the block row itself; a column may repeat in a row, and then its blocks add. `live`: loads differ between row groups.
All inputs are finite; a program needn't handle non-finite values.
Results may differ from a plain program's by a relative error of at most 0.0028.
Values may be sent and summed in bfloat16 or wider, within the bound.
A program may use at most 128 MiB of HBM per device.

v0:
```python
import jax
import jax.numpy as jnp
from jax import lax
from jax.sharding import PartitionSpec as P

REACH = 16
STEPS = 4


def padded(cells, sides, width):
    for axis, dim in sides:
        count = lax.axis_size(axis)
        ends = count - 1
        head = lax.slice_in_dim(cells, 0, width, axis=dim)
        tail = lax.slice_in_dim(cells, cells.shape[dim] - width, cells.shape[dim], axis=dim)
        cells = jnp.concatenate(
            [
                lax.ppermute(tail, axis, [(i, (i + 1) % count) for i in range(ends)]),
                cells,
                lax.ppermute(head, axis, [((i + 1) % count, i) for i in range(ends)]),
            ],
            axis=dim,
        )
    return cells


def complex_parts(out):
    real_part = out[:, 0, :, 0] - out[:, 1, :, 1]
    imag_part = out[:, 0, :, 1] + out[:, 1, :, 0]
    return jnp.stack([real_part, imag_part], axis=2)


def body(start_vec, left_vec, hamil, cols, live):
    row_blocks, slot_count = cols.shape
    block_size = hamil.shape[-1]
    base = lax.axis_index("rows") * row_blocks
    panel_index = cols - base + REACH
    mask_bf = (jnp.arange(slot_count)[None, :] < live).astype(jnp.bfloat16)
    scale = 1.0 / (2.0 * block_size * row_blocks) ** 0.5
    current = start_vec
    previous = start_vec
    table = [jnp.sum(left_vec * current, axis=(0, 1))]
    for step in range(STEPS):
        extended = padded(current.astype(jnp.bfloat16), (("rows", 0),), REACH * block_size)
        all_cols = extended.shape[2]
        blocks = extended.reshape(-1, block_size, 2, all_cols)
        panels = jnp.take(blocks, panel_index, axis=0) * mask_bf[:, :, None, None, None]
        out = jnp.einsum("bkqij,bkjpc->bqipc", hamil, panels, preferred_element_type=jnp.float32)
        summed = lax.psum(
            complex_parts(out).reshape(row_blocks * block_size, 2, all_cols), "section"
        )
        fresh = summed if step == 0 else 2.0 * summed - previous
        previous, current = (current, fresh)
        table.append(jnp.sum(left_vec * current, axis=(0, 1)))
    partial_value = jnp.stack(table, axis=0)
    moments = lax.psum(partial_value, "rows") * scale
    return (moments, current, previous)


def solution(mesh):
    return jax.shard_map(
        body,
        mesh=mesh,
        in_specs=(
            P("rows", None, None),
            P("rows", None, None),
            P("rows", "section", None, None, None),
            P("rows", "section"),
            P("rows", "section"),
        ),
        out_specs=(P(), P("rows", None, None), P("rows", None, None)),
        check_vma=False,
    )
```

profile of v0, /device:TPU:0, one launch (start us, length us, event | category | flops | bytes accessed | tf_op | source)
XLA Modules:
  0.0 1040.7 jit_solution(10793872942615279801)
XLA Ops:
  9.6 3.7 collective-permute-start
  15.9 4.4 collective-permute-done.1
  20.3 3.4 pad_maximum_fusion
  26.8 8.3 gather_fusion
  35.1 10.4 %fusion.12 = f32[16,2,128,2,256]{4,2,1,3,0:T(8,128)} fusion(bf16[16,4,128,2,256]{4,2,3,1,0:T(8,128)(2,1)} %bitcast.79, pred[16,4]{1,0:T(8,128)(4,1)S(1)} %copy.76, bf16[16,4]{1,0:T(8,128)(2,1)S(1)} %fusion.28, bf16[16,4,2,128,128]{4,3,2,1,0:T(8,128)(2,1)} %param.9), kind=kOutput, calls=%fused_computation.37 | convolution fusion | flops 2155872256 | bytes 20971712 | tf_op jit(solution)/shard_map/bkqij,bkjpc->bqipc/dot_general | solution.py:48
  45.5 4.1 slice_subtract_fusion.3
  52.0 196.5 %all-reduce.5.cloned.1.call-done = f32[2048,2,256]{2,0,1:T(8,128)} async-done(((f32[2048,2,256]{2,0,1:T(8,128)}), f32[2048,2,256]{2,0,1:T(8,128)}) %all-reduce.5.cloned.1.call-update) | async-done | bytes 4194320 | tf_op jit(solution)/shard_map/psum | solution.py:49
  256.4 3.6 collective-permute-done.3
  260.0 13.9 %pad_maximum_fusion.1 = bf16[6144,2,256]{2,0,1:T(8,128)(2,1)S(1)} fusion(bf16[2048,2,256]{2,0,1:T(8,128)(2,1)S(1)} %collective-permute-done.3, bf16[2048,2,256]{2,0,1:T(8,128)(2,1)S(1)} %convert_element_type.21, bf16[2048,2,256]{2,0,1:T(8,128)(2,1)S(1)} %collective-permute-done.2), kind=kLoop, calls=%fused_computation.21 | loop fusion | flops 18874368 | bytes 12582912 | tf_op jit(solution)/shard_map/concatenate | solution.py:16
  277.0 8.3 gather_fusion.1
  285.3 10.4 %fusion.15 = f32[16,2,128,2,256]{4,2,1,3,0:T(8,128)} fusion(bf16[16,4,128,2,256]{4,2,3,1,0:T(8,128)(2,1)} %bitcast.80, pred[16,4]{1,0:T(8,128)(4,1)S(1)} %copy.76, bf16[16,4]{1,0:T(8,128)(2,1)S(1)} %fusion.28, bf16[16,4,2,128,128]{4,3,2,1,0:T(8,128)(2,1)} %param.9), kind=kOutput, calls=%fused_computation.38 | convolution fusion | flops 2155872256 | bytes 20971712 | tf_op jit(solution)/shard_map/bkqij,bkjpc->bqipc/dot_general | solution.py:48
  295.8 4.1 slice_subtract_fusion.2
  302.2 194.3 %all-reduce.7.cloned.1.call-done = f32[2048,2,256]{2,0,1:T(8,128)} async-done(((f32[2048,2,256]{2,0,1:T(8,128)}), f32[2048,2,256]{2,0,1:T(8,128)}) %all-reduce.7.cloned.1.call-update) | async-done | bytes 4194320 | tf_op jit(solution)/shard_map/psum | solution.py:49
  496.5 4.1 fusion.29
  506.1 3.6 collective-permute-done.5
  509.7 14.0 %pad_maximum_fusion.2 = bf16[6144,2,256]{2,0,1:T(8,128)(2,1)S(1)} fusion(bf16[2048,2,256]{2,0,1:T(8,128)(2,1)S(1)} %collective-permute-done.5, bf16[2048,2,256]{2,0,1:T(8,128)(2,1)S(1)} %fusion.29, bf16[2048,2,256]{2,0,1:T(8,128)(2,1)S(1)} %collective-permute-done.4), kind=kLoop, calls=%fused_computation.22 | loop fusion | flops 18874368 | bytes 12582912 | tf_op jit(solution)/shard_map/concatenate | solution.py:16
  526.8 8.3 gather_fusion.2
  535.1 10.4 %fusion.18 = f32[16,2,128,2,256]{4,2,1,3,0:T(8,128)} fusion(bf16[16,4,128,2,256]{4,2,3,1,0:T(8,128)(2,1)} %bitcast.81, pred[16,4]{1,0:T(8,128)(4,1)S(1)} %copy.76, bf16[16,4]{1,0:T(8,128)(2,1)S(1)} %fusion.28, bf16[16,4,2,128,128]{4,3,2,1,0:T(8,128)(2,1)} %param.9), kind=kOutput, calls=%fused_computation.39 | convolution fusion | flops 2155872256 | bytes 20971712 | tf_op jit(solution)/shard_map/bkqij,bkjpc->bqipc/dot_general | solution.py:48
  545.5 4.1 slice_subtract_fusion.1
  552.0 194.3 %all-reduce.9.cloned.1.call-done = f32[2048,2,256]{2,0,1:T(8,128)} async-done(((f32[2048,2,256]{2,0,1:T(8,128)}), f32[2048,2,256]{2,0,1:T(8,128)}) %all-reduce.9.cloned.1.call-update) | async-done | bytes 4194320 | tf_op jit(solution)/shard_map/psum | solution.py:49
  746.3 6.1 fusion.30
  757.9 3.6 collective-permute-done.7
  761.5 13.8 %pad_maximum_fusion.3 = bf16[6144,2,256]{2,0,1:T(8,128)(2,1)S(1)} fusion(bf16[2048,2,256]{2,0,1:T(8,128)(2,1)S(1)} %collective-permute-done.7, bf16[2048,2,256]{2,0,1:T(8,128)(2,1)S(1)} %get-tuple-element.12, bf16[2048,2,256]{2,0,1:T(8,128)(2,1)S(1)} %collective-permute-done.6), kind=kLoop, calls=%fused_computation.23 | loop fusion | flops 18874368 | bytes 12582912 | tf_op jit(solution)/shard_map/concatenate | solution.py:16
  778.4 8.3 gather_fusion.3
  786.7 10.4 %fusion.21 = f32[16,2,128,2,256]{4,2,1,3,0:T(8,128)} fusion(bf16[16,4,128,2,256]{4,2,3,1,0:T(8,128)(2,1)} %bitcast.78, pred[16,4]{1,0:T(8,128)(4,1)S(1)} %copy.76, bf16[16,4]{1,0:T(8,128)(2,1)S(1)} %fusion.28, bf16[16,4,2,128,128]{4,3,2,1,0:T(8,128)(2,1)} %param.9), kind=kOutput, calls=%fused_computation.40 | convolution fusion | flops 2155872256 | bytes 20971712 | tf_op jit(solution)/shard_map/bkqij,bkjpc->bqipc/dot_general | solution.py:48
  797.2 4.1 slice_subtract_fusion
  803.5 6.6 multiply_reduce_fusion.4
  810.2 12.4 %copy.103 = f32[2048,2,256]{2,1,0:T(2,128)} copy(f32[2048,2,256]{2,0,1:T(8,128)S(1)} %copy-done) | data formatting | bytes 8388608
  822.5 175.4 %all-reduce.11.cloned.1.call-done = f32[2048,2,256]{2,0,1:T(8,128)} async-done(((f32[2048,2,256]{2,0,1:T(8,128)}), f32[2048,2,256]{2,0,1:T(8,128)}) %all-reduce.11.cloned.1.call-update) | async-done | bytes 4194320 | tf_op jit(solution)/shard_map/psum | solution.py:49
  997.9 9.4 multiply_reduce_fusion
  1007.3 12.2 %copy.102 = f32[2048,2,256]{2,1,0:T(2,128)} copy(f32[2048,2,256]{2,0,1:T(8,128)S(1)} %get-tuple-element.11) | data formatting | bytes 8388608
  1019.5 13.9 %psum.39 = f32[5,256]{1,0:T(8,128)S(1)} all-reduce(f32[5,256]{1,0:T(8,128)S(1)} %stack.47), channel_id=1, replica_groups=mesh['rows'=8,'section'=4] {'rows'}, use_global_device_ids=true, to_apply=%region_9.11 | all-reduce | flops 1280 | bytes 10240 | tf_op jit(solution)/shard_map/psum | solution.py:56
  (43 shorter events, 46.3 us)
Async XLA Ops:
  7.2 7.5 copy-start.1
  7.2 7.7 copy-start.2
  7.2 241.3 %all-reduce.5.cloned.1.call-start = ((), (), s32[]{:S(2)}) async-start(), calls=%async_computation | async-start | bytes 8388608 | tf_op jit(solution)/shard_map/psum | solution.py:49
  9.6 6.3 collective-permute-start
  13.3 7.0 collective-permute-start.1
  51.9 444.6 %all-reduce.7.cloned.1.call-start = ((), (), s32[]{:S(2)}) async-start(), calls=%async_computation.1 | async-start | bytes 8388608 | tf_op jit(solution)/shard_map/psum | solution.py:49
  250.9 5.5 collective-permute-start.2
  252.8 7.2 collective-permute-start.3
  302.2 444.1 %all-reduce.9.cloned.1.call-start = ((), (), s32[]{:S(2)}) async-start(), calls=%async_computation.2 | async-start | bytes 8388608 | tf_op jit(solution)/shard_map/psum | solution.py:49
  500.6 5.5 collective-permute-start.4
  502.5 7.2 collective-permute-start.5
  551.9 446.0 %all-reduce.11.cloned.1.call-start = ((), (), s32[]{:S(2)}) async-start(), calls=%async_computation.3 | async-start | bytes 8388608 | tf_op jit(solution)/shard_map/psum | solution.py:49
  752.4 5.5 collective-permute-start.6
  754.3 7.2 collective-permute-start.7
  803.5 6.6 copy-start
Sparse Core Ops, SparseCore 0:
  52.1 196.4 all-reduce.4
  302.3 194.2 all-reduce.6
  552.1 194.1 all-reduce.8
  803.6 194.2 all-reduce.10
where the time goes:
time: 1050 us; the launch traced here: 1040 us
  waiting for transfers between devices  783 us (75%)
  other arithmetic  99.7 us (9%)
  local copies, waits for them, and re-layouts  73 us (7%)
  matrix products  41.7 us (4%)
  starting transfers between devices  15.4 us (1%)
  between operations  14.2 us (1%)
  blocking collectives  13.9 us (1%)
    psum x4, waiting for transfers between devices, body(): lax.psum(complex_parts(out).reshape(row_blocks * block_size, 2, all_cols)...  761 us
    concatenate x4, other arithmetic, padded(): jnp.concatenate([lax.ppermute(tail, axis, [(i, (i + 1) % count) for i in...  45 us
    dot_general x4, matrix products, body(): jnp.einsum('bkqij,bkjpc->bqipc', hamil, panels, preferred_element_type=jn...  41.7 us
    gather x4, local copies, waits for them, and re-layouts, body(): jnp.take(blocks, panel_index, axis=0) * mask_bf[:, :, None, None, None]  33.2 us
    unnamed x9, local copies, waits for them, and re-layouts  27 us
  transfers between devices with their start and end apart: 12, of which 12 were waited for; matrix products, arithmetic and copies ran while one was open for 2% of the time, Pallas kernels for 0%

commit v1 on v0

--- a/solution.py
+++ b/solution.py
@@ -46,9 +46,9 @@
         blocks = extended.reshape(-1, block_size, 2, all_cols)
         panels = jnp.take(blocks, panel_index, axis=0) * mask_bf[:, :, None, None, None]
         out = jnp.einsum("bkqij,bkjpc->bqipc", hamil, panels, preferred_element_type=jnp.float32)
-        summed = lax.psum(
-            complex_parts(out).reshape(row_blocks * block_size, 2, all_cols), "section"
-        )
+        own = complex_parts(out).reshape(row_blocks * block_size, 2, all_cols)
+        parts = lax.all_gather(own, "section")
+        summed = jnp.sum(parts, axis=0)
         fresh = summed if step == 0 else 2.0 * summed - previous
         previous, current = (current, fresh)
         table.append(jnp.sum(left_vec * current, axis=(0, 1)))

time: 1050 us -> 1610 us (1.53)
  waiting for transfers between devices: 783 us -> 1310 us
  other arithmetic: 99.7 us -> 137 us
    all_gather x0 -> x4, waiting for transfers between devices: none -> 1280 us  [body(): parts = lax.all_gather(own, 'section')]
    psum x4 -> x0, waiting for transfers between devices: 761 us -> none  [body(): lax.psum(complex_parts(out).reshape(row_blocks * block_size, 2, all_cols)...]
    reduce_sum x0 -> x4, other arithmetic: none -> 37.8 us  [body(): summed = jnp.sum(parts, axis=0)]
  transfers between devices with their start and end apart: 12 -> 12, of which waited for: 12 -> 12; matrix products, arithmetic and copies ran while one was open for 2% -> 1% of each run, Pallas kernels for 0% -> 0%
where the time goes in v1:
time: 1610 us; the launch traced here: 1600 us
  waiting for transfers between devices  1310 us (81%)
  other arithmetic  137 us (9%)
  local copies, waits for them, and re-layouts  73 us (5%)
  matrix products  41.7 us (3%)
    all_gather x4, waiting for transfers between devices, body(): parts = lax.all_gather(own, 'section')  1280 us
    concatenate x4, other arithmetic, padded(): jnp.concatenate([lax.ppermute(tail, axis, [(i, (i + 1) % count) for i in...  45 us
    dot_general x4, matrix products, body(): jnp.einsum('bkqij,bkjpc->bqipc', hamil, panels, preferred_element_type=jn...  41.7 us
    reduce_sum x4, other arithmetic, body(): summed = jnp.sum(parts, axis=0)  37.8 us
    gather x4, local copies, waits for them, and re-layouts, body(): jnp.take(blocks, panel_index, axis=0) * mask_bf[:, :, None, None, None]  33.2 us
  transfers between devices with their start and end apart: 12, of which 12 were waited for; matrix products, arithmetic and copies ran while one was open for 1% of the time, Pallas kernels for 0%

profile of v1, /device:TPU:0, one launch (start us, length us, event | category | flops | bytes accessed | tf_op | source)
XLA Modules:
  0.0 1603.4 jit_solution(3834370951352924915)
XLA Ops:
  9.6 3.7 collective-permute-start
  15.9 4.4 collective-permute-done.1
  26.8 8.3 gather_fusion
  35.1 10.4 fusion.12
  45.5 4.1 slice_subtract_fusion.3
  52.0 328.3 %all-gather.5.cloned.1.call-done = f32[4,2048,2,256]{3,1,2,0:T(8,128)} async-done(((f32[1,2048,2,256]{3,1,2,0:T(8,128)}), f32[4,2048,2,256]{3,1,2,0:T(8,128)}) %all-gather.5.cloned.1.call-update) | async-done | bytes 16777232 | tf_op jit(solution)/shard_map/all_gather | solution.py:50
  380.3 9.5 reduce_sum.82
  401.2 13.9 pad_maximum_fusion.1
  418.3 8.3 gather_fusion.1
  426.6 10.4 fusion.15
  437.0 4.1 slice_subtract_fusion.2
  443.9 324.9 %all-gather.7.cloned.1.call-done = f32[4,2048,2,256]{3,1,2,0:T(8,128)} async-done(((f32[1,2048,2,256]{3,1,2,0:T(8,128)}), f32[4,2048,2,256]{3,1,2,0:T(8,128)}) %all-gather.7.cloned.1.call-update) | async-done | bytes 16777232 | tf_op jit(solution)/shard_map/all_gather | solution.py:50
  768.8 9.4 reduce_sum.84
  778.2 4.1 fusion.29
  791.3 14.0 pad_maximum_fusion.2
  808.4 8.3 gather_fusion.2
  816.7 10.4 fusion.18
  827.1 4.1 slice_subtract_fusion.1
  833.8 325.2 %all-gather.9.cloned.1.call-done = f32[4,2048,2,256]{3,1,2,0:T(8,128)} async-done(((f32[1,2048,2,256]{3,1,2,0:T(8,128)}), f32[4,2048,2,256]{3,1,2,0:T(8,128)}) %all-gather.9.cloned.1.call-update) | async-done | bytes 16777232 | tf_op jit(solution)/shard_map/all_gather | solution.py:50
  1158.9 9.5 reduce_sum.86
  1168.4 6.0 fusion.30
  1183.5 13.8 pad_maximum_fusion.3
  1200.4 8.3 gather_fusion.3
  1208.7 10.4 fusion.21
  1219.1 4.1 slice_subtract_fusion
  1225.5 6.6 multiply_reduce_fusion.4
  1232.1 12.4 copy.107
  1244.6 306.3 %all-gather.11.cloned.1.call-done = f32[4,2048,2,256]{3,1,2,0:T(8,128)} async-done(((f32[1,2048,2,256]{3,1,2,0:T(8,128)}), f32[4,2048,2,256]{3,1,2,0:T(8,128)}) %all-gather.11.cloned.1.call-update) | async-done | bytes 16777232 | tf_op jit(solution)/shard_map/all_gather | solution.py:50
  1550.9 9.4 reduce_sum.88
  1560.3 9.4 multiply_reduce_fusion
  1569.7 12.2 copy.106
  1581.9 14.1 psum.7
  (47 shorter events, 60.9 us)
Async XLA Ops:
  7.2 7.5 copy-start.1
  7.2 7.7 copy-start.2
  7.2 373.1 %all-gather.5.cloned.1.call-start = ((), (), s32[]{:S(2)}) async-start(), calls=%async_computation | async-start | bytes 20971520 | tf_op jit(solution)/shard_map/all_gather | solution.py:50
  9.6 6.3 collective-permute-start
  13.3 7.0 collective-permute-start.1
  51.9 716.9 %all-gather.7.cloned.1.call-start = ((), (), s32[]{:S(2)}) async-start(), calls=%async_computation.1 | async-start | bytes 20971520 | tf_op jit(solution)/shard_map/all_gather | solution.py:50
  392.2 5.7 collective-permute-start.2
  394.3 7.0 collective-permute-start.3
  443.4 715.5 %all-gather.9.cloned.1.call-start = ((), (), s32[]{:S(2)}) async-start(), calls=%async_computation.2 | async-start | bytes 20971520 | tf_op jit(solution)/shard_map/all_gather | solution.py:50
  782.3 5.7 collective-permute-start.4
  784.4 7.0 collective-permute-start.5
  833.5 717.4 %all-gather.11.cloned.1.call-start = ((), (), s32[]{:S(2)}) async-start(), calls=%async_computation.3 | async-start | bytes 20971520 | tf_op jit(solution)/shard_map/all_gather | solution.py:50
  1174.4 5.7 collective-permute-start.6
  1176.5 7.0 collective-permute-start.7
  1225.5 6.6 copy-start
Sparse Core Ops, SparseCore 0:
  52.1 328.2 all-gather.4
  443.5 325.2 all-gather.6
  833.7 325.2 all-gather.8
  1225.6 325.2 all-gather.10
